TPU v7x, 512 devices: a whole 4x4x16 slice. The times are simulated.
512 devices in a mesh: span: 32 (over z, core), head: 16 (over y, x).
Axes of the slice: x: 4, y: 4, z: 16, core: 2. Of those that a mesh axis runs over, the one named last changes fastest.
Arguments:
- query_rows: bfloat16 [5120, 6144], P('span', 'head'), may hold values from -6 to 6
- key_rows: bfloat16 [5120, 6144], P('span', 'head'), may hold values from -6 to 6
- value_rows: bfloat16 [5120, 6144], P('span', 'head'), may hold values from -6 to 6
- block_mask: int32 [32, 32], P('span'), may hold values from 0 to 1, as said below
- noise_level: int32 [32], P('span'), may hold values from 0 to 15
- level_gain: float32 [16, 6144], P(None, 'head'), may hold values from 0.5 to 2
- out_weight: bfloat16 [6144, 6144], P('head', 'span'), may hold values from -0.625 to 0.625
Outputs:
- update_rows: bfloat16 [5120, 6144], P('span', 'head')
Inputs may be any that keep to these rules, and one draw needn't show every extreme that they name: block_mask[i, i] is 1, block_mask[i, i - 1] is 1 for i > 0, and block_mask[i, j] is 0 for j > i; farther below the diagonal entries are 0 or 1.
All inputs are finite; a program needn't handle non-finite values.
Results may differ from a plain program's by a relative error of at most 0.02.
Values may be sent and summed in bfloat16 or wider, within the bound.
A program may use at most 64 MiB of HBM per device.

v0:
```python
import jax
import jax.numpy as jnp
from jax import lax
from jax.sharding import PartitionSpec as P

HD = 128


NEG_FILL = -1e30


def shifted(value, axis, by):
    length = lax.axis_size(axis)
    pairs = [(i, i + by) for i in range(length) if 0 <= i + by < length]
    return lax.ppermute(value, axis, pairs)


def allowed_rows(source_span, mask_row, span_count):
    matches = source_span[:, None] == jnp.arange(span_count, dtype=jnp.int32)[None, :]
    return jnp.sum(jnp.where(matches, mask_row[None, :], 0), axis=1) > 0


def attend(query_heads, key_piece, value_piece, allowed, softmax_state):
    running_max, row_total, weighted = softmax_state
    count_rows = key_piece.shape[0]
    heads_here = query_heads.shape[1]
    key_heads = key_piece.reshape(count_rows, heads_here, HD)
    value_heads = value_piece.reshape(count_rows, heads_here, HD)
    logits = jnp.einsum(
        "thd,khd->thk", query_heads, key_heads, preferred_element_type=jnp.float32
    ) * HD ** (-0.5)
    logits = jnp.where(allowed[None, None, :], logits, NEG_FILL)
    new_max = jnp.maximum(running_max, jnp.max(logits, axis=2))
    probs = jnp.where(allowed[None, None, :], jnp.exp(logits - new_max[:, :, None]), 0.0)
    factor = jnp.exp(running_max - new_max)
    row_total = row_total * factor + jnp.sum(probs, axis=2)
    weighted = weighted * factor[:, :, None] + jnp.einsum(
        "thk,khd->thd", probs.astype(jnp.bfloat16), value_heads, preferred_element_type=jnp.float32
    )
    return (new_max, row_total, weighted)


def on_device(query_rows, key_rows, value_rows, block_mask, noise_level, level_gain, out_weight):
    tok_rows, row_width = query_rows.shape
    heads_here = row_width // HD
    span_count = block_mask.shape[1]
    position = lax.axis_index("span")
    mask_row = block_mask[0]
    query_heads = query_rows.reshape(tok_rows, heads_here, HD)
    start_state = (
        jnp.full((tok_rows, heads_here), NEG_FILL, jnp.float32),
        jnp.zeros((tok_rows, heads_here), jnp.float32),
        jnp.zeros((tok_rows, heads_here, HD), jnp.float32),
    )
    own_source = jnp.full((tok_rows,), position, jnp.int32)
    softmax_state = attend(
        query_heads,
        key_rows,
        value_rows,
        allowed_rows(own_source, mask_row, span_count),
        start_state,
    )

    def advance(step_index, carried):
        panel_pair, inner_state = carried
        panel_pair = shifted(panel_pair, "span", 1)
        source = jnp.full((tok_rows,), position - step_index - 1, jnp.int32)
        inner_state = attend(
            query_heads,
            panel_pair[0],
            panel_pair[1],
            allowed_rows(source, mask_row, span_count),
            inner_state,
        )
        return (panel_pair, inner_state)

    carried = lax.fori_loop(
        0, lax.axis_size("span") - 1, advance, (jnp.stack([key_rows, value_rows]), softmax_state)
    )
    softmax_state = carried[1]
    attended = (
        (softmax_state[2] / softmax_state[1][:, :, None])
        .reshape(tok_rows, row_width)
        .astype(jnp.bfloat16)
    )
    partial_terms = jnp.dot(
        attended,
        lax.all_gather(out_weight, "span", axis=1, tiled=True),
        preferred_element_type=jnp.float32,
    )
    summed = lax.psum_scatter(
        partial_terms.astype(jnp.bfloat16), "head", scatter_dimension=1, tiled=True
    ).astype(jnp.float32)
    level_count = level_gain.shape[0]
    onehot = (noise_level[0] == jnp.arange(level_count, dtype=jnp.int32)).astype(jnp.float32)
    gain_row = jnp.dot(onehot, level_gain, precision=lax.Precision.HIGHEST)
    return (summed * gain_row[None, :]).astype(jnp.bfloat16)


def solution(mesh):
    return jax.shard_map(
        on_device,
        mesh=mesh,
        in_specs=(
            P("span", "head"),
            P("span", "head"),
            P("span", "head"),
            P("span", None),
            P("span"),
            P(None, "head"),
            P("head", "span"),
        ),
        out_specs=P("span", "head"),
        check_vma=False,
    )
```

profile of v0, /device:TPU:6, one launch (start us, length us, event | category | flops | bytes accessed | tf_op | source)
XLA Modules:
  0.0 434.6 jit_solution(5608248928093617970)
XLA Ops:
  11.7 283.8 %while.21 = (s32[]{:T(128)}, bf16[2,160,384]{2,1,0:T(8,128)(2,1)S(1)}, f32[160,3]{0,1:T(4,128)S(1)}, f32[160,3]{0,1:T(4,128)S(1)}, f32[160,3,128]{2,0,1:T(8,128)...) while((s32[]{:T(128)}, ...), condition=%wide.region_7.8_spmd, body=%wide.region_3.7_spmd.sunk | while | flops 40146916 | bytes 4272361 | solution.py:77
  23.9 6.4 %collective-permute-start = (bf16[2,160,384]{2,1,0:T(8,128)(2,1)S(1)}, bf16[2,160,384]{2,1,0:T(8,128)(2,1)S(1)}, u32[]{:S(2)}, u32[]{:S(2)}) collective-permute-start(bf16[2,160,384]{2,1,0:T(8,128)(2,1)S(1)} %get-tuple-element.328), channel_id=1, source_target_pairs={{0,16},{16,32},{32,48},{48,64},{64,80},{80,96},{96,112},{112,128},... | collective-permute-start | bytes 737288 | tf_op jit(solution)/shard_map/while/body/eval_jaxpr/ppermute | solution.py:15
  32.4 6.7 %collective-permute-start = (bf16[2,160,384]{2,1,0:T(8,128)(2,1)S(1)}, bf16[2,160,384]{2,1,0:T(8,128)(2,1)S(1)}, u32[]{:S(2)}, u32[]{:S(2)}) collective-permute-start(bf16[2,160,384]{2,1,0:T(8,128)(2,1)S(1)} %get-tuple-element.328), channel_id=1, source_target_pairs={{0,16},{16,32},{32,48},{48,64},{64,80},{80,96},{96,112},{112,128},... | collective-permute-start | bytes 737288 | tf_op jit(solution)/shard_map/while/body/eval_jaxpr/ppermute | solution.py:15
  41.2 8.5 %collective-permute-start = (bf16[2,160,384]{2,1,0:T(8,128)(2,1)S(1)}, bf16[2,160,384]{2,1,0:T(8,128)(2,1)S(1)}, u32[]{:S(2)}, u32[]{:S(2)}) collective-permute-start(bf16[2,160,384]{2,1,0:T(8,128)(2,1)S(1)} %get-tuple-element.328), channel_id=1, source_target_pairs={{0,16},{16,32},{32,48},{48,64},{64,80},{80,96},{96,112},{112,128},... | collective-permute-start | bytes 737288 | tf_op jit(solution)/shard_map/while/body/eval_jaxpr/ppermute | solution.py:15
  51.8 8.7 %collective-permute-start = (bf16[2,160,384]{2,1,0:T(8,128)(2,1)S(1)}, bf16[2,160,384]{2,1,0:T(8,128)(2,1)S(1)}, u32[]{:S(2)}, u32[]{:S(2)}) collective-permute-start(bf16[2,160,384]{2,1,0:T(8,128)(2,1)S(1)} %get-tuple-element.328), channel_id=1, source_target_pairs={{0,16},{16,32},{32,48},{48,64},{64,80},{80,96},{96,112},{112,128},... | collective-permute-start | bytes 737288 | tf_op jit(solution)/shard_map/while/body/eval_jaxpr/ppermute | solution.py:15
  62.7 8.1 %collective-permute-start = (bf16[2,160,384]{2,1,0:T(8,128)(2,1)S(1)}, bf16[2,160,384]{2,1,0:T(8,128)(2,1)S(1)}, u32[]{:S(2)}, u32[]{:S(2)}) collective-permute-start(bf16[2,160,384]{2,1,0:T(8,128)(2,1)S(1)} %get-tuple-element.328), channel_id=1, source_target_pairs={{0,16},{16,32},{32,48},{48,64},{64,80},{80,96},{96,112},{112,128},... | collective-permute-start | bytes 737288 | tf_op jit(solution)/shard_map/while/body/eval_jaxpr/ppermute | solution.py:15
  72.9 8.6 %collective-permute-start = (bf16[2,160,384]{2,1,0:T(8,128)(2,1)S(1)}, bf16[2,160,384]{2,1,0:T(8,128)(2,1)S(1)}, u32[]{:S(2)}, u32[]{:S(2)}) collective-permute-start(bf16[2,160,384]{2,1,0:T(8,128)(2,1)S(1)} %get-tuple-element.328), channel_id=1, source_target_pairs={{0,16},{16,32},{32,48},{48,64},{64,80},{80,96},{96,112},{112,128},... | collective-permute-start | bytes 737288 | tf_op jit(solution)/shard_map/while/body/eval_jaxpr/ppermute | solution.py:15
  83.6 6.8 %collective-permute-start = (bf16[2,160,384]{2,1,0:T(8,128)(2,1)S(1)}, bf16[2,160,384]{2,1,0:T(8,128)(2,1)S(1)}, u32[]{:S(2)}, u32[]{:S(2)}) collective-permute-start(bf16[2,160,384]{2,1,0:T(8,128)(2,1)S(1)} %get-tuple-element.328), channel_id=1, source_target_pairs={{0,16},{16,32},{32,48},{48,64},{64,80},{80,96},{96,112},{112,128},... | collective-permute-start | bytes 737288 | tf_op jit(solution)/shard_map/while/body/eval_jaxpr/ppermute | solution.py:15
  92.5 6.5 %collective-permute-start = (bf16[2,160,384]{2,1,0:T(8,128)(2,1)S(1)}, bf16[2,160,384]{2,1,0:T(8,128)(2,1)S(1)}, u32[]{:S(2)}, u32[]{:S(2)}) collective-permute-start(bf16[2,160,384]{2,1,0:T(8,128)(2,1)S(1)} %get-tuple-element.328), channel_id=1, source_target_pairs={{0,16},{16,32},{32,48},{48,64},{64,80},{80,96},{96,112},{112,128},... | collective-permute-start | bytes 737288 | tf_op jit(solution)/shard_map/while/body/eval_jaxpr/ppermute | solution.py:15
  109.7 6.4 %collective-permute-start = (bf16[2,160,384]{2,1,0:T(8,128)(2,1)S(1)}, bf16[2,160,384]{2,1,0:T(8,128)(2,1)S(1)}, u32[]{:S(2)}, u32[]{:S(2)}) collective-permute-start(bf16[2,160,384]{2,1,0:T(8,128)(2,1)S(1)} %get-tuple-element.328), channel_id=1, source_target_pairs={{0,16},{16,32},{32,48},{48,64},{64,80},{80,96},{96,112},{112,128},... | collective-permute-start | bytes 737288 | tf_op jit(solution)/shard_map/while/body/eval_jaxpr/ppermute | solution.py:15
  169.4 7.1 %collective-permute-start = (bf16[2,160,384]{2,1,0:T(8,128)(2,1)S(1)}, bf16[2,160,384]{2,1,0:T(8,128)(2,1)S(1)}, u32[]{:S(2)}, u32[]{:S(2)}) collective-permute-start(bf16[2,160,384]{2,1,0:T(8,128)(2,1)S(1)} %get-tuple-element.328), channel_id=1, source_target_pairs={{0,16},{16,32},{32,48},{48,64},{64,80},{80,96},{96,112},{112,128},... | collective-permute-start | bytes 737288 | tf_op jit(solution)/shard_map/while/body/eval_jaxpr/ppermute | solution.py:15
  178.6 7.6 %collective-permute-start = (bf16[2,160,384]{2,1,0:T(8,128)(2,1)S(1)}, bf16[2,160,384]{2,1,0:T(8,128)(2,1)S(1)}, u32[]{:S(2)}, u32[]{:S(2)}) collective-permute-start(bf16[2,160,384]{2,1,0:T(8,128)(2,1)S(1)} %get-tuple-element.328), channel_id=1, source_target_pairs={{0,16},{16,32},{32,48},{48,64},{64,80},{80,96},{96,112},{112,128},... | collective-permute-start | bytes 737288 | tf_op jit(solution)/shard_map/while/body/eval_jaxpr/ppermute | solution.py:15
  188.3 7.6 %collective-permute-start = (bf16[2,160,384]{2,1,0:T(8,128)(2,1)S(1)}, bf16[2,160,384]{2,1,0:T(8,128)(2,1)S(1)}, u32[]{:S(2)}, u32[]{:S(2)}) collective-permute-start(bf16[2,160,384]{2,1,0:T(8,128)(2,1)S(1)} %get-tuple-element.328), channel_id=1, source_target_pairs={{0,16},{16,32},{32,48},{48,64},{64,80},{80,96},{96,112},{112,128},... | collective-permute-start | bytes 737288 | tf_op jit(solution)/shard_map/while/body/eval_jaxpr/ppermute | solution.py:15
  198.1 7.6 %collective-permute-start = (bf16[2,160,384]{2,1,0:T(8,128)(2,1)S(1)}, bf16[2,160,384]{2,1,0:T(8,128)(2,1)S(1)}, u32[]{:S(2)}, u32[]{:S(2)}) collective-permute-start(bf16[2,160,384]{2,1,0:T(8,128)(2,1)S(1)} %get-tuple-element.328), channel_id=1, source_target_pairs={{0,16},{16,32},{32,48},{48,64},{64,80},{80,96},{96,112},{112,128},... | collective-permute-start | bytes 737288 | tf_op jit(solution)/shard_map/while/body/eval_jaxpr/ppermute | solution.py:15
  207.8 7.6 %collective-permute-start = (bf16[2,160,384]{2,1,0:T(8,128)(2,1)S(1)}, bf16[2,160,384]{2,1,0:T(8,128)(2,1)S(1)}, u32[]{:S(2)}, u32[]{:S(2)}) collective-permute-start(bf16[2,160,384]{2,1,0:T(8,128)(2,1)S(1)} %get-tuple-element.328), channel_id=1, source_target_pairs={{0,16},{16,32},{32,48},{48,64},{64,80},{80,96},{96,112},{112,128},... | collective-permute-start | bytes 737288 | tf_op jit(solution)/shard_map/while/body/eval_jaxpr/ppermute | solution.py:15
  217.6 7.6 %collective-permute-start = (bf16[2,160,384]{2,1,0:T(8,128)(2,1)S(1)}, bf16[2,160,384]{2,1,0:T(8,128)(2,1)S(1)}, u32[]{:S(2)}, u32[]{:S(2)}) collective-permute-start(bf16[2,160,384]{2,1,0:T(8,128)(2,1)S(1)} %get-tuple-element.328), channel_id=1, source_target_pairs={{0,16},{16,32},{32,48},{48,64},{64,80},{80,96},{96,112},{112,128},... | collective-permute-start | bytes 737288 | tf_op jit(solution)/shard_map/while/body/eval_jaxpr/ppermute | solution.py:15
  227.3 7.6 %collective-permute-start = (bf16[2,160,384]{2,1,0:T(8,128)(2,1)S(1)}, bf16[2,160,384]{2,1,0:T(8,128)(2,1)S(1)}, u32[]{:S(2)}, u32[]{:S(2)}) collective-permute-start(bf16[2,160,384]{2,1,0:T(8,128)(2,1)S(1)} %get-tuple-element.328), channel_id=1, source_target_pairs={{0,16},{16,32},{32,48},{48,64},{64,80},{80,96},{96,112},{112,128},... | collective-permute-start | bytes 737288 | tf_op jit(solution)/shard_map/while/body/eval_jaxpr/ppermute | solution.py:15
  237.0 7.6 %collective-permute-start = (bf16[2,160,384]{2,1,0:T(8,128)(2,1)S(1)}, bf16[2,160,384]{2,1,0:T(8,128)(2,1)S(1)}, u32[]{:S(2)}, u32[]{:S(2)}) collective-permute-start(bf16[2,160,384]{2,1,0:T(8,128)(2,1)S(1)} %get-tuple-element.328), channel_id=1, source_target_pairs={{0,16},{16,32},{32,48},{48,64},{64,80},{80,96},{96,112},{112,128},... | collective-permute-start | bytes 737288 | tf_op jit(solution)/shard_map/while/body/eval_jaxpr/ppermute | solution.py:15
  246.8 7.6 %collective-permute-start = (bf16[2,160,384]{2,1,0:T(8,128)(2,1)S(1)}, bf16[2,160,384]{2,1,0:T(8,128)(2,1)S(1)}, u32[]{:S(2)}, u32[]{:S(2)}) collective-permute-start(bf16[2,160,384]{2,1,0:T(8,128)(2,1)S(1)} %get-tuple-element.328), channel_id=1, source_target_pairs={{0,16},{16,32},{32,48},{48,64},{64,80},{80,96},{96,112},{112,128},... | collective-permute-start | bytes 737288 | tf_op jit(solution)/shard_map/while/body/eval_jaxpr/ppermute | solution.py:15
  256.5 7.6 %collective-permute-start = (bf16[2,160,384]{2,1,0:T(8,128)(2,1)S(1)}, bf16[2,160,384]{2,1,0:T(8,128)(2,1)S(1)}, u32[]{:S(2)}, u32[]{:S(2)}) collective-permute-start(bf16[2,160,384]{2,1,0:T(8,128)(2,1)S(1)} %get-tuple-element.328), channel_id=1, source_target_pairs={{0,16},{16,32},{32,48},{48,64},{64,80},{80,96},{96,112},{112,128},... | collective-permute-start | bytes 737288 | tf_op jit(solution)/shard_map/while/body/eval_jaxpr/ppermute | solution.py:15
  266.3 7.6 %collective-permute-start = (bf16[2,160,384]{2,1,0:T(8,128)(2,1)S(1)}, bf16[2,160,384]{2,1,0:T(8,128)(2,1)S(1)}, u32[]{:S(2)}, u32[]{:S(2)}) collective-permute-start(bf16[2,160,384]{2,1,0:T(8,128)(2,1)S(1)} %get-tuple-element.328), channel_id=1, source_target_pairs={{0,16},{16,32},{32,48},{48,64},{64,80},{80,96},{96,112},{112,128},... | collective-permute-start | bytes 737288 | tf_op jit(solution)/shard_map/while/body/eval_jaxpr/ppermute | solution.py:15
  276.0 7.6 %collective-permute-start = (bf16[2,160,384]{2,1,0:T(8,128)(2,1)S(1)}, bf16[2,160,384]{2,1,0:T(8,128)(2,1)S(1)}, u32[]{:S(2)}, u32[]{:S(2)}) collective-permute-start(bf16[2,160,384]{2,1,0:T(8,128)(2,1)S(1)} %get-tuple-element.328), channel_id=1, source_target_pairs={{0,16},{16,32},{32,48},{48,64},{64,80},{80,96},{96,112},{112,128},... | collective-permute-start | bytes 737288 | tf_op jit(solution)/shard_map/while/body/eval_jaxpr/ppermute | solution.py:15
  285.8 7.6 %collective-permute-start = (bf16[2,160,384]{2,1,0:T(8,128)(2,1)S(1)}, bf16[2,160,384]{2,1,0:T(8,128)(2,1)S(1)}, u32[]{:S(2)}, u32[]{:S(2)}) collective-permute-start(bf16[2,160,384]{2,1,0:T(8,128)(2,1)S(1)} %get-tuple-element.328), channel_id=1, source_target_pairs={{0,16},{16,32},{32,48},{48,64},{64,80},{80,96},{96,112},{112,128},... | collective-permute-start | bytes 737288 | tf_op jit(solution)/shard_map/while/body/eval_jaxpr/ppermute | solution.py:15
  303.2 122.8 %reduce-scatter.4.cloned.1.call-done = bf16[384,160]{1,0:T(8,128)(2,1)} async-done(((bf16[6144,160]{1,0:T(8,128)(2,1)}), bf16[384,160]{1,0:T(8,128)(2,1)}) %reduce-scatter.4.cloned.1.call-update) | async-done | bytes 122896
  (467 shorter events, 129.9 us)
Async XLA Ops:
  6.5 289.0 %all-gather.2.cloned.1.call-start = ((), (), s32[]{:S(2)}) async-start(), calls=%async_computation.1 | async-start | bytes 4866048 | tf_op jit(solution)/shard_map/all_gather | solution.py:88
  7.3 418.8 %reduce-scatter.4.cloned.1.call-start = ((), (), s32[]{:S(2)}) async-start(), calls=%async_computation.2 | async-start | bytes 3342336
  23.9 7.5 %collective-permute-start = (bf16[2,160,384]{2,1,0:T(8,128)(2,1)S(1)}, bf16[2,160,384]{2,1,0:T(8,128)(2,1)S(1)}, u32[]{:S(2)}, u32[]{:S(2)}) collective-permute-start(bf16[2,160,384]{2,1,0:T(8,128)(2,1)S(1)} %get-tuple-element.328), channel_id=1, source_target_pairs={{0,16},{16,32},{32,48},{48,64},{64,80},{80,96},{96,112},{112,128},... | collective-permute-start | bytes 737288 | tf_op jit(solution)/shard_map/while/body/eval_jaxpr/ppermute | solution.py:15
  32.4 7.8 %collective-permute-start = (bf16[2,160,384]{2,1,0:T(8,128)(2,1)S(1)}, bf16[2,160,384]{2,1,0:T(8,128)(2,1)S(1)}, u32[]{:S(2)}, u32[]{:S(2)}) collective-permute-start(bf16[2,160,384]{2,1,0:T(8,128)(2,1)S(1)} %get-tuple-element.328), channel_id=1, source_target_pairs={{0,16},{16,32},{32,48},{48,64},{64,80},{80,96},{96,112},{112,128},... | collective-permute-start | bytes 737288 | tf_op jit(solution)/shard_map/while/body/eval_jaxpr/ppermute | solution.py:15
  41.2 9.6 %collective-permute-start = (bf16[2,160,384]{2,1,0:T(8,128)(2,1)S(1)}, bf16[2,160,384]{2,1,0:T(8,128)(2,1)S(1)}, u32[]{:S(2)}, u32[]{:S(2)}) collective-permute-start(bf16[2,160,384]{2,1,0:T(8,128)(2,1)S(1)} %get-tuple-element.328), channel_id=1, source_target_pairs={{0,16},{16,32},{32,48},{48,64},{64,80},{80,96},{96,112},{112,128},... | collective-permute-start | bytes 737288 | tf_op jit(solution)/shard_map/while/body/eval_jaxpr/ppermute | solution.py:15
  51.8 9.9 %collective-permute-start = (bf16[2,160,384]{2,1,0:T(8,128)(2,1)S(1)}, bf16[2,160,384]{2,1,0:T(8,128)(2,1)S(1)}, u32[]{:S(2)}, u32[]{:S(2)}) collective-permute-start(bf16[2,160,384]{2,1,0:T(8,128)(2,1)S(1)} %get-tuple-element.328), channel_id=1, source_target_pairs={{0,16},{16,32},{32,48},{48,64},{64,80},{80,96},{96,112},{112,128},... | collective-permute-start | bytes 737288 | tf_op jit(solution)/shard_map/while/body/eval_jaxpr/ppermute | solution.py:15
  62.7 9.2 %collective-permute-start = (bf16[2,160,384]{2,1,0:T(8,128)(2,1)S(1)}, bf16[2,160,384]{2,1,0:T(8,128)(2,1)S(1)}, u32[]{:S(2)}, u32[]{:S(2)}) collective-permute-start(bf16[2,160,384]{2,1,0:T(8,128)(2,1)S(1)} %get-tuple-element.328), channel_id=1, source_target_pairs={{0,16},{16,32},{32,48},{48,64},{64,80},{80,96},{96,112},{112,128},... | collective-permute-start | bytes 737288 | tf_op jit(solution)/shard_map/while/body/eval_jaxpr/ppermute | solution.py:15
  72.9 9.7 %collective-permute-start = (bf16[2,160,384]{2,1,0:T(8,128)(2,1)S(1)}, bf16[2,160,384]{2,1,0:T(8,128)(2,1)S(1)}, u32[]{:S(2)}, u32[]{:S(2)}) collective-permute-start(bf16[2,160,384]{2,1,0:T(8,128)(2,1)S(1)} %get-tuple-element.328), channel_id=1, source_target_pairs={{0,16},{16,32},{32,48},{48,64},{64,80},{80,96},{96,112},{112,128},... | collective-permute-start | bytes 737288 | tf_op jit(solution)/shard_map/while/body/eval_jaxpr/ppermute | solution.py:15
  83.6 7.9 %collective-permute-start = (bf16[2,160,384]{2,1,0:T(8,128)(2,1)S(1)}, bf16[2,160,384]{2,1,0:T(8,128)(2,1)S(1)}, u32[]{:S(2)}, u32[]{:S(2)}) collective-permute-start(bf16[2,160,384]{2,1,0:T(8,128)(2,1)S(1)} %get-tuple-element.328), channel_id=1, source_target_pairs={{0,16},{16,32},{32,48},{48,64},{64,80},{80,96},{96,112},{112,128},... | collective-permute-start | bytes 737288 | tf_op jit(solution)/shard_map/while/body/eval_jaxpr/ppermute | solution.py:15
  92.5 7.6 %collective-permute-start = (bf16[2,160,384]{2,1,0:T(8,128)(2,1)S(1)}, bf16[2,160,384]{2,1,0:T(8,128)(2,1)S(1)}, u32[]{:S(2)}, u32[]{:S(2)}) collective-permute-start(bf16[2,160,384]{2,1,0:T(8,128)(2,1)S(1)} %get-tuple-element.328), channel_id=1, source_target_pairs={{0,16},{16,32},{32,48},{48,64},{64,80},{80,96},{96,112},{112,128},... | collective-permute-start | bytes 737288 | tf_op jit(solution)/shard_map/while/body/eval_jaxpr/ppermute | solution.py:15
  109.7 7.5 %collective-permute-start = (bf16[2,160,384]{2,1,0:T(8,128)(2,1)S(1)}, bf16[2,160,384]{2,1,0:T(8,128)(2,1)S(1)}, u32[]{:S(2)}, u32[]{:S(2)}) collective-permute-start(bf16[2,160,384]{2,1,0:T(8,128)(2,1)S(1)} %get-tuple-element.328), channel_id=1, source_target_pairs={{0,16},{16,32},{32,48},{48,64},{64,80},{80,96},{96,112},{112,128},... | collective-permute-start | bytes 737288 | tf_op jit(solution)/shard_map/while/body/eval_jaxpr/ppermute | solution.py:15
  169.4 8.2 %collective-permute-start = (bf16[2,160,384]{2,1,0:T(8,128)(2,1)S(1)}, bf16[2,160,384]{2,1,0:T(8,128)(2,1)S(1)}, u32[]{:S(2)}, u32[]{:S(2)}) collective-permute-start(bf16[2,160,384]{2,1,0:T(8,128)(2,1)S(1)} %get-tuple-element.328), channel_id=1, source_target_pairs={{0,16},{16,32},{32,48},{48,64},{64,80},{80,96},{96,112},{112,128},... | collective-permute-start | bytes 737288 | tf_op jit(solution)/shard_map/while/body/eval_jaxpr/ppermute | solution.py:15
  178.6 8.7 %collective-permute-start = (bf16[2,160,384]{2,1,0:T(8,128)(2,1)S(1)}, bf16[2,160,384]{2,1,0:T(8,128)(2,1)S(1)}, u32[]{:S(2)}, u32[]{:S(2)}) collective-permute-start(bf16[2,160,384]{2,1,0:T(8,128)(2,1)S(1)} %get-tuple-element.328), channel_id=1, source_target_pairs={{0,16},{16,32},{32,48},{48,64},{64,80},{80,96},{96,112},{112,128},... | collective-permute-start | bytes 737288 | tf_op jit(solution)/shard_map/while/body/eval_jaxpr/ppermute | solution.py:15
  188.3 8.7 %collective-permute-start = (bf16[2,160,384]{2,1,0:T(8,128)(2,1)S(1)}, bf16[2,160,384]{2,1,0:T(8,128)(2,1)S(1)}, u32[]{:S(2)}, u32[]{:S(2)}) collective-permute-start(bf16[2,160,384]{2,1,0:T(8,128)(2,1)S(1)} %get-tuple-element.328), channel_id=1, source_target_pairs={{0,16},{16,32},{32,48},{48,64},{64,80},{80,96},{96,112},{112,128},... | collective-permute-start | bytes 737288 | tf_op jit(solution)/shard_map/while/body/eval_jaxpr/ppermute | solution.py:15
  198.1 8.7 %collective-permute-start = (bf16[2,160,384]{2,1,0:T(8,128)(2,1)S(1)}, bf16[2,160,384]{2,1,0:T(8,128)(2,1)S(1)}, u32[]{:S(2)}, u32[]{:S(2)}) collective-permute-start(bf16[2,160,384]{2,1,0:T(8,128)(2,1)S(1)} %get-tuple-element.328), channel_id=1, source_target_pairs={{0,16},{16,32},{32,48},{48,64},{64,80},{80,96},{96,112},{112,128},... | collective-permute-start | bytes 737288 | tf_op jit(solution)/shard_map/while/body/eval_jaxpr/ppermute | solution.py:15
  207.8 8.7 %collective-permute-start = (bf16[2,160,384]{2,1,0:T(8,128)(2,1)S(1)}, bf16[2,160,384]{2,1,0:T(8,128)(2,1)S(1)}, u32[]{:S(2)}, u32[]{:S(2)}) collective-permute-start(bf16[2,160,384]{2,1,0:T(8,128)(2,1)S(1)} %get-tuple-element.328), channel_id=1, source_target_pairs={{0,16},{16,32},{32,48},{48,64},{64,80},{80,96},{96,112},{112,128},... | collective-permute-start | bytes 737288 | tf_op jit(solution)/shard_map/while/body/eval_jaxpr/ppermute | solution.py:15
  217.6 8.7 %collective-permute-start = (bf16[2,160,384]{2,1,0:T(8,128)(2,1)S(1)}, bf16[2,160,384]{2,1,0:T(8,128)(2,1)S(1)}, u32[]{:S(2)}, u32[]{:S(2)}) collective-permute-start(bf16[2,160,384]{2,1,0:T(8,128)(2,1)S(1)} %get-tuple-element.328), channel_id=1, source_target_pairs={{0,16},{16,32},{32,48},{48,64},{64,80},{80,96},{96,112},{112,128},... | collective-permute-start | bytes 737288 | tf_op jit(solution)/shard_map/while/body/eval_jaxpr/ppermute | solution.py:15
  227.3 8.7 %collective-permute-start = (bf16[2,160,384]{2,1,0:T(8,128)(2,1)S(1)}, bf16[2,160,384]{2,1,0:T(8,128)(2,1)S(1)}, u32[]{:S(2)}, u32[]{:S(2)}) collective-permute-start(bf16[2,160,384]{2,1,0:T(8,128)(2,1)S(1)} %get-tuple-element.328), channel_id=1, source_target_pairs={{0,16},{16,32},{32,48},{48,64},{64,80},{80,96},{96,112},{112,128},... | collective-permute-start | bytes 737288 | tf_op jit(solution)/shard_map/while/body/eval_jaxpr/ppermute | solution.py:15
  237.0 8.7 %collective-permute-start = (bf16[2,160,384]{2,1,0:T(8,128)(2,1)S(1)}, bf16[2,160,384]{2,1,0:T(8,128)(2,1)S(1)}, u32[]{:S(2)}, u32[]{:S(2)}) collective-permute-start(bf16[2,160,384]{2,1,0:T(8,128)(2,1)S(1)} %get-tuple-element.328), channel_id=1, source_target_pairs={{0,16},{16,32},{32,48},{48,64},{64,80},{80,96},{96,112},{112,128},... | collective-permute-start | bytes 737288 | tf_op jit(solution)/shard_map/while/body/eval_jaxpr/ppermute | solution.py:15
  246.8 8.7 %collective-permute-start = (bf16[2,160,384]{2,1,0:T(8,128)(2,1)S(1)}, bf16[2,160,384]{2,1,0:T(8,128)(2,1)S(1)}, u32[]{:S(2)}, u32[]{:S(2)}) collective-permute-start(bf16[2,160,384]{2,1,0:T(8,128)(2,1)S(1)} %get-tuple-element.328), channel_id=1, source_target_pairs={{0,16},{16,32},{32,48},{48,64},{64,80},{80,96},{96,112},{112,128},... | collective-permute-start | bytes 737288 | tf_op jit(solution)/shard_map/while/body/eval_jaxpr/ppermute | solution.py:15
  256.5 8.7 %collective-permute-start = (bf16[2,160,384]{2,1,0:T(8,128)(2,1)S(1)}, bf16[2,160,384]{2,1,0:T(8,128)(2,1)S(1)}, u32[]{:S(2)}, u32[]{:S(2)}) collective-permute-start(bf16[2,160,384]{2,1,0:T(8,128)(2,1)S(1)} %get-tuple-element.328), channel_id=1, source_target_pairs={{0,16},{16,32},{32,48},{48,64},{64,80},{80,96},{96,112},{112,128},... | collective-permute-start | bytes 737288 | tf_op jit(solution)/shard_map/while/body/eval_jaxpr/ppermute | solution.py:15
  266.3 8.7 %collective-permute-start = (bf16[2,160,384]{2,1,0:T(8,128)(2,1)S(1)}, bf16[2,160,384]{2,1,0:T(8,128)(2,1)S(1)}, u32[]{:S(2)}, u32[]{:S(2)}) collective-permute-start(bf16[2,160,384]{2,1,0:T(8,128)(2,1)S(1)} %get-tuple-element.328), channel_id=1, source_target_pairs={{0,16},{16,32},{32,48},{48,64},{64,80},{80,96},{96,112},{112,128},... | collective-permute-start | bytes 737288 | tf_op jit(solution)/shard_map/while/body/eval_jaxpr/ppermute | solution.py:15
  276.0 8.7 %collective-permute-start = (bf16[2,160,384]{2,1,0:T(8,128)(2,1)S(1)}, bf16[2,160,384]{2,1,0:T(8,128)(2,1)S(1)}, u32[]{:S(2)}, u32[]{:S(2)}) collective-permute-start(bf16[2,160,384]{2,1,0:T(8,128)(2,1)S(1)} %get-tuple-element.328), channel_id=1, source_target_pairs={{0,16},{16,32},{32,48},{48,64},{64,80},{80,96},{96,112},{112,128},... | collective-permute-start | bytes 737288 | tf_op jit(solution)/shard_map/while/body/eval_jaxpr/ppermute | solution.py:15
  285.8 8.7 %collective-permute-start = (bf16[2,160,384]{2,1,0:T(8,128)(2,1)S(1)}, bf16[2,160,384]{2,1,0:T(8,128)(2,1)S(1)}, u32[]{:S(2)}, u32[]{:S(2)}) collective-permute-start(bf16[2,160,384]{2,1,0:T(8,128)(2,1)S(1)} %get-tuple-element.328), channel_id=1, source_target_pairs={{0,16},{16,32},{32,48},{48,64},{64,80},{80,96},{96,112},{112,128},... | collective-permute-start | bytes 737288 | tf_op jit(solution)/shard_map/while/body/eval_jaxpr/ppermute | solution.py:15
  (11 other events, 67.7 us)
Sparse Core Ops, SparseCore 0:
  9.5 80.7 all-gather.1
  302.5 123.4 reduce-scatter.3
where the time goes:
time: 436 us; the launch traced here: 435 us
  starting transfers between devices  218 us (50%)
  waiting for transfers between devices  134 us (31%)
  other arithmetic  30.7 us (7%)
  matrix products  27.6 us (6%)
  between operations  14.2 us (3%)
  local copies, waits for them, and re-layouts  7.96 us (2%)
    ppermute x31, starting transfers between devices, shifted(): return lax.ppermute(value, axis, pairs)  218 us
    unnamed x3, waiting for transfers between devices  124 us
    reduce_sum x32, other arithmetic, allowed_rows(): return jnp.sum(jnp.where(matches, mask_row[None, :], 0), axis=1) > 0  23.9 us
    dot_general x32, matrix products, attend(): jnp.einsum('thk,khd->thd', probs.astype(jnp.bfloat16), value_heads, prefe...  13.8 us
    ppermute x31, waiting for transfers between devices, shifted(): return lax.ppermute(value, axis, pairs)  10.2 us
    dot_general x32, matrix products, attend(): jnp.einsum('thd,khd->thk', query_heads, key_heads, preferred_element_type...  9.49 us
  transfers between devices with their start and end apart: 33, of which 32 were waited for; matrix products, arithmetic and copies ran while one was open for 13% of the time, Pallas kernels for 0%

commit v1 on v0

v1 whole, which is shorter than its diff:
```python
import functools
import math

import jax
import jax.numpy as jnp
from jax import lax
from jax.experimental import pallas as pl
from jax.experimental.pallas import tpu as pltpu
from jax.sharding import PartitionSpec as P

MESH = pl.DeviceIdType.MESH
HD = 128
NZ = 16
NX = 4
ROWS = 160
HALF = ROWS // 2
WIDTH = 384
HEADS = WIDTH // HD
NEG = -1e30
SCORE_SCALE = math.log2(math.e) / math.sqrt(HD)
KEY, VALUE, WEIGHT = 0, 1, 2


def kernel(
    q_hbm, k_hbm, v_hbm, mask_ref, level_ref, gain_hbm, w_hbm, out_ref,
    q_ref, gain_ref, kbuf, vbuf, wall, row_max, row_sum, acc, att, part,
    tx1, rx1, tx2, rx2, tx3, rx3, mid,
    ring_s, ring_r, sib_s, sib_r, s1, r1, s2, r2, s3, r3, load,
):
    span = lax.axis_index("span")
    group = lax.axis_index("head")
    z, core = span // 2, span % 2
    y, x = group // NX, group % NX
    z_up = (lax.rem(z + 1, NZ) * 2 + core, group)
    z_down = (lax.rem(z + NZ - 1, NZ) * 2 + core, group)
    sibling = (z * 2 + 1 - core, group)
    toward = [z_up, z_down]

    def in_plane(axis, by):
        if axis == 0:
            return (span, y * NX + lax.rem(x + by, NX))
        return (span, lax.rem(y + by, NX) * NX + x)

    own = [(k_hbm, kbuf.at[pl.ds(0, ROWS)]), (v_hbm, vbuf.at[pl.ds(0, ROWS)]),
           (w_hbm, wall.at[0, core]), (q_hbm, q_ref), (gain_hbm, gain_ref)]
    loads = [pltpu.make_async_copy(src, dst, load.at[i]) for i, (src, dst) in enumerate(own)]
    for copy in loads:
        copy.start()

    barrier = pltpu.get_barrier_semaphore()
    peers = [z_up, z_down, sibling] + [in_plane(a, b) for a in (0, 1) for b in (1, 2, 3)]
    for peer in peers:
        pl.semaphore_signal(barrier, inc=1, device_id=peer, device_id_type=MESH)
    pl.semaphore_wait(barrier, len(peers))

    def chunk_base(way, dist):
        return pl.multiple_of(320 + (dist - 1) * 640 + way * 320, 160)

    def chunk(kind, way, dist, own_ring=True):
        if kind == WEIGHT:
            slot = dist if isinstance(dist, int) and dist == 0 else dist + way * 8
            return wall.at[slot, core if own_ring else 1 - core]
        buf = kbuf if kind == KEY else vbuf
        sub = 0 if own_ring else 1
        if isinstance(dist, int) and dist == 0:
            return buf.at[pl.ds(sub * ROWS, ROWS)]
        return buf.at[pl.ds(pl.multiple_of(chunk_base(way, dist) + sub * ROWS, 160), ROWS)]

    def ring_copy(kind, way, dist):
        return pltpu.make_async_remote_copy(
            src_ref=chunk(kind, way, dist),
            dst_ref=chunk(kind, way, dist + 1),
            send_sem=ring_s.at[kind, way, dist],
            recv_sem=ring_r.at[kind, way, dist + 1],
            device_id=toward[way],
            device_id_type=MESH,
        )

    def first_hop(kind, way):
        return pltpu.make_async_remote_copy(
            src_ref=own[kind][0],
            dst_ref=chunk(kind, way, 1),
            send_sem=ring_s.at[kind, way, 0],
            recv_sem=ring_r.at[kind, way, 1],
            device_id=toward[way],
            device_id_type=MESH,
        )

    def far_copy(kind, way):
        src, dst = chunk(kind, way, 7), chunk(kind, 0, 8)
        if kind == WEIGHT:
            src, dst = src.at[pl.ds(way * 96, 96)], dst.at[pl.ds(way * 96, 96)]
        return pltpu.make_async_remote_copy(
            src_ref=src,
            dst_ref=dst,
            send_sem=ring_s.at[kind, way, 7],
            recv_sem=ring_r.at[kind, way, 8],
            device_id=toward[way],
            device_id_type=MESH,
        )

    def arrival(kind, way, dist):
        landed = chunk(kind, way, dist)
        return pltpu.make_async_remote_copy(
            src_ref=landed,
            dst_ref=landed,
            send_sem=ring_s.at[kind, way, dist - 1],
            recv_sem=ring_r.at[kind, way, dist],
            device_id=toward[way],
            device_id_type=MESH,
        )

    def sibling_copy(kind, way, dist):
        dst = chunk(kind, way, dist, kind == WEIGHT)
        return pltpu.make_async_remote_copy(
            src_ref=chunk(kind, way, dist),
            dst_ref=dst,
            send_sem=sib_s.at[kind, way, dist],
            recv_sem=sib_r.at[kind, way, dist],
            device_id=sibling,
            device_id_type=MESH,
        )

    def sibling_arrival(kind, way, dist):
        landed = chunk(kind, way, dist, False)
        return pltpu.make_async_remote_copy(
            src_ref=landed,
            dst_ref=landed,
            send_sem=sib_s.at[kind, way, dist],
            recv_sem=sib_r.at[kind, way, dist],
            device_id=sibling,
            device_id_type=MESH,
        )

    for kind in (KEY, VALUE, WEIGHT):
        for way in (0, 1):
            first_hop(kind, way).start()
    for kind in (KEY, VALUE, WEIGHT):
        loads[kind].wait()
        sibling_copy(kind, 0, 0).start()
    loads[3].wait()
    loads[4].wait()

    row_max[...] = jnp.full_like(row_max, NEG)
    row_sum[...] = jnp.zeros_like(row_sum)
    acc[...] = jnp.zeros_like(acc)

    def visible(chip, which):
        return mask_ref[0, lax.rem(chip + 2 * NZ, NZ) * 2 + which]

    def attend(base, seen):
        count = len(seen) * ROWS
        lane_span = lax.broadcasted_iota(jnp.int32, (1, count), 1) // ROWS
        bias = jnp.zeros((1, count), jnp.float32)
        for place, flag in enumerate(seen):
            bias = jnp.where(lane_span == place, jnp.where(flag > 0, 0.0, NEG), bias)
        for head in range(HEADS):
            cols = slice(head * HD, (head + 1) * HD)
            scores = lax.dot_general(
                q_ref[:, cols], kbuf[pl.ds(base, count), cols], (((1,), (1,)), ((), ())),
                preferred_element_type=jnp.float32,
            )
            scores = scores * SCORE_SCALE + bias
            old_max = row_max[head][:, 0:1]
            new_max = jnp.maximum(old_max, jnp.max(scores, axis=1, keepdims=True))
            probs = jnp.exp2(scores - new_max)
            factor = jnp.exp2(old_max - new_max)
            total = row_sum[head][:, 0:1] * factor + jnp.sum(probs, axis=1, keepdims=True)
            row_max[head] = jnp.broadcast_to(new_max, (ROWS, HD))
            row_sum[head] = jnp.broadcast_to(total, (ROWS, HD))
            acc[head] = acc[head] * factor + jnp.dot(
                probs.astype(jnp.bfloat16), vbuf[pl.ds(base, count), cols],
                preferred_element_type=jnp.float32,
            )

    sibling_arrival(KEY, 0, 0).wait_recv()
    sibling_arrival(VALUE, 0, 0).wait_recv()
    attend(0, [visible(z, core), visible(z, 1 - core)])

    def hop(dist, _):
        for kind in (KEY, VALUE, WEIGHT):
            for way in (0, 1):
                arrival(kind, way, dist).wait_recv()

                @pl.when(dist < 7)
                def _():
                    ring_copy(kind, way, dist).start()

                if kind != WEIGHT:
                    send_far = way == kind

                    @pl.when(dist == 7)
                    def _():
                        if send_far:
                            far_copy(kind, way).start()
                else:

                    @pl.when(dist == 7)
                    def _():
                        far_copy(kind, way).start()

                sibling_copy(kind, way, dist).start()
        for kind in (KEY, VALUE):
            for way in (0, 1):
                sibling_arrival(kind, way, dist).wait_recv()
        attend(
            chunk_base(0, dist),
            [
                visible(z - dist, core), visible(z - dist, 1 - core),
                visible(z + dist, core), visible(z + dist, 1 - core),
            ],
        )
        return 0

    lax.fori_loop(1, 8, hop, 0)

    far_copy(KEY, 0).wait_recv()
    sibling_copy(KEY, 0, 8).start()
    far_copy(VALUE, 1).wait_recv()
    sibling_copy(VALUE, 0, 8).start()
    sibling_arrival(KEY, 0, 8).wait_recv()
    sibling_arrival(VALUE, 0, 8).wait_recv()
    attend(chunk_base(0, 8), [visible(z - 8, core), visible(z - 8, 1 - core)])
    for head in range(HEADS):
        att[:, head * HD:(head + 1) * HD] = (acc[head] / row_sum[head]).astype(jnp.bfloat16)

    for way in (0, 1):
        far_copy(WEIGHT, way).wait_recv()
    sibling_copy(WEIGHT, 0, 8).start()
    sibling_arrival(WEIGHT, 0, 0).wait_recv()

    def weights_in(dist, _):
        for way in (0, 1):
            sibling_arrival(WEIGHT, way, dist).wait_recv()
        return 0

    lax.fori_loop(1, 8, weights_in, 0)
    sibling_arrival(WEIGHT, 0, 8).wait_recv()

    def project(column, row):
        block = row * NX + column
        away = lax.rem(z - block + NZ, NZ)
        slot = jnp.where(away <= 8, away, 24 - away)
        part[block] = lax.dot_general(
            att[...], wall[slot].reshape(WIDTH, WIDTH), (((1,), (1,)), ((), ())),
            preferred_element_type=jnp.float32,
        )

    here = [x, y]

    def block_at(half, lead, other):
        return other * NX + lead if half == 0 else lead * NX + other

    def share(half, lead, by):
        other = lax.rem(here[1 - half] + by, NX)
        return part[block_at(half, lead, other), half * HALF:(half + 1) * HALF, :]

    def send(src, dst, ssem, rsem, axis, by):
        return pltpu.make_async_remote_copy(
            src_ref=src, dst_ref=dst, send_sem=ssem, recv_sem=rsem,
            device_id=in_plane(axis, by), device_id_type=MESH,
        )

    def first_copy(half, way, by):
        at = (half, way, by)
        return send(tx1.at[at], rx1.at[at], s1.at[at], r1.at[at], half, 1 + 2 * way)

    def second_copy(half, way, by):
        at = (half, way, by)
        return send(tx2.at[at], rx2.at[at], s2.at[at], r2.at[at], half, 1 + 2 * way)

    def third_copy(half, by):
        at = (half, by - 1)
        return send(tx3.at[at], rx3.at[at], s3.at[at], r3.at[at], 1 - half, by)

    far_places = ((1, 0), (2, 3))

    for by in range(NX):
        project(lax.rem(x + 2, NX), lax.rem(y + by, NX))
        if by != 2:
            project(lax.rem(x + by, NX), lax.rem(y + 2, NX))
    for place in (0, 1):
        for half in (0, 1):
            far = lax.rem(here[half] + 2, NX)
            for way in (0, 1):
                by = far_places[way][place]
                tx1[half, way, by] = share(half, far, by).astype(jnp.bfloat16)
                first_copy(half, way, by).start()
    for column in (0, 1, 3):
        for row in (0, 1, 3):
            project(lax.rem(x + column, NX), lax.rem(y + row, NX))

    def near(half, way):
        return lax.rem(here[half] + 1 + 2 * way, NX)

    for place in (0, 1):
        for half in (0, 1):
            for way in (0, 1):
                by = far_places[1 - way][place]
                tx2[half, way, by] = share(half, near(half, way), by).astype(jnp.bfloat16)
                second_copy(half, way, by).start()
    for place in (0, 1):
        for half in (0, 1):
            for way in (0, 1):
                by = far_places[way][place]
                first_copy(half, way, by).wait_recv()
                term = share(half, near(half, way), by) + rx1[half, way, by].astype(jnp.float32)
                tx2[half, way, by] = term.astype(jnp.bfloat16)
                second_copy(half, way, by).start()
    for by in (2, 1, 3, 0):
        for half in (0, 1):
            for way in (0, 1):
                second_copy(half, way, by).wait_recv()
            total = (
                share(half, here[half], by)
                + rx2[half, 0, by].astype(jnp.float32)
                + rx2[half, 1, by].astype(jnp.float32)
            )
            if by:
                tx3[half, by - 1] = total.astype(jnp.bfloat16)
                third_copy(half, by).start()
            else:
                mid[half] = total

    levels = gain_ref.shape[0]
    chosen = lax.broadcasted_iota(jnp.int32, (levels, 1), 0) == level_ref[0]
    gain_row = jnp.sum(jnp.where(chosen, gain_ref[...], 0.0), axis=0, keepdims=True)
    for half in (0, 1):
        total = mid[half]
        for by in (1, 3, 2):
            third_copy(half, by).wait_recv()
            total = total + rx3[half, by - 1].astype(jnp.float32)
        out_ref[half * HALF:(half + 1) * HALF, :] = (total * gain_row).astype(jnp.bfloat16)

    for kind in (KEY, VALUE, WEIGHT):
        sibling_copy(kind, 0, 0).wait_send()
        sibling_copy(kind, 0, 8).wait_send()
        for way in (0, 1):
            first_hop(kind, way).wait_send()
            if kind == WEIGHT or kind == way:
                far_copy(kind, way).wait_send()

    def left(dist, _):
        for kind in (KEY, VALUE, WEIGHT):
            for way in (0, 1):
                sibling_copy(kind, way, dist).wait_send()

                @pl.when(dist < 7)
                def _():
                    ring_copy(kind, way, dist).wait_send()

        return 0

    lax.fori_loop(1, 8, left, 0)
    for half in (0, 1):
        for way in (0, 1):
            for by in range(NX):
                if by in far_places[way]:
                    first_copy(half, way, by).wait_send()
                second_copy(half, way, by).wait_send()
        for by in (1, 2, 3):
            third_copy(half, by).wait_send()


def on_device(query_rows, key_rows, value_rows, block_mask, noise_level, level_gain, out_weight):
    vmem = pl.BlockSpec(memory_space=pltpu.VMEM)
    hbm = pl.BlockSpec(memory_space=pl.ANY)
    smem = pl.BlockSpec(memory_space=pltpu.SMEM)
    dma = pltpu.SemaphoreType.DMA
    tokens = 2 * NZ * ROWS

    def b16(*shape):
        return pltpu.VMEM(shape, jnp.bfloat16)

    def f32(*shape):
        return pltpu.VMEM(shape, jnp.float32)

    return pl.pallas_call(
        kernel,
        out_shape=jax.ShapeDtypeStruct((ROWS, WIDTH), jnp.bfloat16),
        in_specs=[hbm, hbm, hbm, smem, smem, hbm, hbm],
        out_specs=vmem,
        scratch_shapes=[
            b16(ROWS, WIDTH), f32(*level_gain.shape),
            b16(tokens, WIDTH), b16(tokens, WIDTH), b16(NZ, 2, 192, WIDTH),
            f32(HEADS, ROWS, HD), f32(HEADS, ROWS, HD), f32(HEADS, ROWS, HD),
            b16(ROWS, WIDTH), f32(NX * NX, ROWS, WIDTH),
            b16(2, 2, 4, HALF, WIDTH), b16(2, 2, 4, HALF, WIDTH),
            b16(2, 2, 4, HALF, WIDTH), b16(2, 2, 4, HALF, WIDTH),
            b16(2, 3, HALF, WIDTH), b16(2, 3, HALF, WIDTH),
            f32(2, HALF, WIDTH),
            dma((3, 2, 8)), dma((3, 2, 9)), dma((3, 2, 9)), dma((3, 2, 9)),
            dma((2, 2, 4)), dma((2, 2, 4)), dma((2, 2, 4)), dma((2, 2, 4)), dma((2, 3)), dma((2, 3)),
            dma((5,)),
        ],
        compiler_params=pltpu.CompilerParams(
            collective_id=0, has_side_effects=True, vmem_limit_bytes=62 << 20
        ),
    )(query_rows, key_rows, value_rows, block_mask, noise_level, level_gain, out_weight.T)


def solution(mesh):
    return jax.shard_map(
        on_device,
        mesh=mesh,
        in_specs=(
            P("span", "head"),
            P("span", "head"),
            P("span", "head"),
            P("span", None),
            P("span"),
            P(None, "head"),
            P("head", "span"),
        ),
        out_specs=P("span", "head"),
        check_vma=False,
    )
```

time: 436 us -> 102 us (0.23)
  starting transfers between devices: 218 us -> 0 us
  waiting for transfers between devices: 134 us -> 0 us
  Pallas kernels: 0 us -> 98.8 us
  other arithmetic: 30.7 us -> 0 us
  matrix products: 27.6 us -> 0 us
  between operations: 14.2 us -> 0.66 us
  local copies, waits for them, and re-layouts: 7.96 us -> 1.56 us
    ppermute x31 -> x0, starting transfers between devices: 218 us -> none  [shifted(): return lax.ppermute(value, axis, pairs)]
    unnamed x3 -> x0, waiting for transfers between devices: 124 us -> none
    pallas_call x0 -> x1, Pallas kernels: none -> 98.8 us  [on_device(): pl.pallas_call(kernel, out_shape=jax.ShapeDtypeStruct((ROWS, WIDTH), jnp....]
    reduce_sum x64 -> x0, other arithmetic: 28 us -> none  [the longest x32 23.9 us: allowed_rows(): return jnp.sum(jnp.where(matches, mask_row[None, :], 0), axis=1) > 0]
    dot_general x66 -> x0, matrix products: 27.6 us -> none  [the longest x32 13.8 us: attend(): jnp.einsum('thk,khd->thd', probs.astype(jnp.bfloat16), value_heads, prefe...]
    ppermute x31 -> x0, waiting for transfers between devices: 10.2 us -> none  [shifted(): return lax.ppermute(value, axis, pairs)]
  transfers between devices with their start and end apart: 33 -> 0, of which waited for: 32 -> 0; matrix products, arithmetic and copies ran while one was open for 13% -> 0% of each run, Pallas kernels for 0% -> 0%
where the time goes in v1:
time: 102 us; the launch traced here: 101 us
  Pallas kernels  98.8 us (97%)
  local copies, waits for them, and re-layouts  1.56 us (2%)
    pallas_call x1, Pallas kernels, on_device(): pl.pallas_call(kernel, out_shape=jax.ShapeDtypeStruct((ROWS, WIDTH), jnp....  98.8 us

profile of v1, /device:TPU:6, one launch (start us, length us, event | category | flops | bytes accessed | tf_op | source)
XLA Modules:
  0.0 101.0 jit_solution(7367451985976605985)
XLA Ops:
  0.7 98.8 %shard_map.73 = bf16[160,384]{1,0:T(8,128)(2,1)} custom-call(bf16[160,384]{1,0:T(8,128)(2,1)} %q_hbm.1, bf16[160,384]{1,0:T(8,128)(2,1)} %k_hbm.1, bf16[160,384]{1,0:T(8,128)(2,1)} %v_hbm.1, s32[1,32]{1,0:T(1,128)} %mask_ref.1, s32[1]{0:T(128)S(6)} %copy.9.level_ref, f32[16,384]{1,0:T(8,128)} %gain_hbm.1, bf16[192,384]{1,0:T(8,128)(2,1)} %bitcast.1), custom_call_target="tpu_custom_call" | custom-call | tf_op jit(solution)/shard_map/pallas_call | solution.py:378
  99.4 1.6 %copy.10 = bf16[160,384]{1,0:T(8,128)(2,1)} copy(bf16[160,384]{1,0:T(8,128)(2,1)} %shard_map.73) | data formatting | bytes 245760

commit v2 on v1

--- a/solution.py
+++ b/solution.py
@@ -178,7 +178,7 @@
     attend(0, [visible(z, core), visible(z, 1 - core)])
 
     def hop(dist, _):
-        for kind in (KEY, VALUE, WEIGHT):
+        for kind in (KEY, VALUE):
             for way in (0, 1):
                 arrival(kind, way, dist).wait_recv()
 
@@ -210,6 +210,28 @@
                 visible(z + dist, core), visible(z + dist, 1 - core),
             ],
         )
+        for kind in (WEIGHT,):
+            for way in (0, 1):
+                arrival(kind, way, dist).wait_recv()
+
+                @pl.when(dist < 7)
+                def _():
+                    ring_copy(kind, way, dist).start()
+
+                if kind != WEIGHT:
+                    send_far = way == kind
+
+                    @pl.when(dist == 7)
+                    def _():
+                        if send_far:
+                            far_copy(kind, way).start()
+                else:
+
+                    @pl.when(dist == 7)
+                    def _():
+                        far_copy(kind, way).start()
+
+                sibling_copy(kind, way, dist).start()
         return 0
 
     lax.fori_loop(1, 8, hop, 0)
@@ -274,39 +296,44 @@
         return send(tx3.at[at], rx3.at[at], s3.at[at], r3.at[at], 1 - half, by)
 
     far_places = ((1, 0), (2, 3))
-
-    for by in range(NX):
-        project(lax.rem(x + 2, NX), lax.rem(y + by, NX))
-        if by != 2:
-            project(lax.rem(x + by, NX), lax.rem(y + 2, NX))
+    near_order = ((2, 1, 3, 0), (1, 2, 3, 0))
+    projected = set()
+
+    def need(column, row):
+        if (column, row) not in projected:
+            projected.add((column, row))
+            project(lax.rem(x + column, NX), lax.rem(y + row, NX))
+
+    def need_share(half, lead_by, by):
+        need(*((lead_by, by) if half == 0 else (by, lead_by)))
+
     for place in (0, 1):
         for half in (0, 1):
             far = lax.rem(here[half] + 2, NX)
             for way in (0, 1):
                 by = far_places[way][place]
+                need_share(half, 2, by)
                 tx1[half, way, by] = share(half, far, by).astype(jnp.bfloat16)
                 first_copy(half, way, by).start()
-    for column in (0, 1, 3):
-        for row in (0, 1, 3):
-            project(lax.rem(x + column, NX), lax.rem(y + row, NX))
 
     def near(half, way):
         return lax.rem(here[half] + 1 + 2 * way, NX)
 
-    for place in (0, 1):
+    for place in range(NX):
         for half in (0, 1):
             for way in (0, 1):
-                by = far_places[1 - way][place]
-                tx2[half, way, by] = share(half, near(half, way), by).astype(jnp.bfloat16)
-                second_copy(half, way, by).start()
-    for place in (0, 1):
-        for half in (0, 1):
-            for way in (0, 1):
-                by = far_places[way][place]
-                first_copy(half, way, by).wait_recv()
-                term = share(half, near(half, way), by) + rx1[half, way, by].astype(jnp.float32)
+                by = near_order[way][place]
+                need_share(half, 1 + 2 * way, by)
+                term = share(half, near(half, way), by)
+                if by in far_places[way]:
+                    first_copy(half, way, by).wait_recv()
+                    term = term + rx1[half, way, by].astype(jnp.float32)
                 tx2[half, way, by] = term.astype(jnp.bfloat16)
                 second_copy(half, way, by).start()
+        if place == 0:
+            for column in range(NX):
+                for row in range(NX):
+                    need(column, row)
     for by in (2, 1, 3, 0):
         for half in (0, 1):
             for way in (0, 1):

time: 102 us -> 101 us (level)
  no operation moved by 1% of the time
where the time goes in v2:
time: 101 us; the launch traced here: 100 us
  Pallas kernels  98.3 us (97%)
  local copies, waits for them, and re-layouts  1.56 us (2%)
    pallas_call x1, Pallas kernels, on_device(): pl.pallas_call(kernel, out_shape=jax.ShapeDtypeStruct((ROWS, WIDTH), jnp....  98.3 us

profile of v2, /device:TPU:6, one launch (start us, length us, event | category | flops | bytes accessed | tf_op | source)
XLA Modules:
  0.0 100.5 jit_solution(9293476149078243784)
XLA Ops:
  0.7 98.3 %shard_map.73 = bf16[160,384]{1,0:T(8,128)(2,1)} custom-call(bf16[160,384]{1,0:T(8,128)(2,1)} %q_hbm.1, bf16[160,384]{1,0:T(8,128)(2,1)} %k_hbm.1, bf16[160,384]{1,0:T(8,128)(2,1)} %v_hbm.1, s32[1,32]{1,0:T(1,128)} %mask_ref.1, s32[1]{0:T(128)S(6)} %copy.9.level_ref, f32[16,384]{1,0:T(8,128)} %gain_hbm.1, bf16[192,384]{1,0:T(8,128)(2,1)} %bitcast.1), custom_call_target="tpu_custom_call" | custom-call | tf_op jit(solution)/shard_map/pallas_call | solution.py:405
  98.9 1.6 %copy.10 = bf16[160,384]{1,0:T(8,128)(2,1)} copy(bf16[160,384]{1,0:T(8,128)(2,1)} %shard_map.73) | data formatting | bytes 245760

commit v3 on v2

--- a/solution.py
+++ b/solution.py
@@ -234,7 +234,8 @@
                 sibling_copy(kind, way, dist).start()
         return 0
 
-    lax.fori_loop(1, 8, hop, 0)
+    for dist in range(1, 8):
+        hop(dist, 0)
 
     far_copy(KEY, 0).wait_recv()
     sibling_copy(KEY, 0, 8).start()
@@ -315,6 +316,28 @@
                 need_share(half, 2, by)
                 tx1[half, way, by] = share(half, far, by).astype(jnp.bfloat16)
                 first_copy(half, way, by).start()
+
+    def ring_left():
+        for kind in (KEY, VALUE, WEIGHT):
+            sibling_copy(kind, 0, 0).wait_send()
+            sibling_copy(kind, 0, 8).wait_send()
+            for way in (0, 1):
+                first_hop(kind, way).wait_send()
+                if kind == WEIGHT or kind == way:
+                    far_copy(kind, way).wait_send()
+
+        def left(dist, _):
+            for kind in (KEY, VALUE, WEIGHT):
+                for way in (0, 1):
+                    sibling_copy(kind, way, dist).wait_send()
+
+                    @pl.when(dist < 7)
+                    def _():
+                        ring_copy(kind, way, dist).wait_send()
+
+            return 0
+
+        lax.fori_loop(1, 8, left, 0)
 
     def near(half, way):
         return lax.rem(here[half] + 1 + 2 * way, NX)
@@ -334,6 +357,7 @@
             for column in range(NX):
                 for row in range(NX):
                     need(column, row)
+            ring_left()
     for by in (2, 1, 3, 0):
         for half in (0, 1):
             for way in (0, 1):
@@ -349,6 +373,13 @@
             else:
                 mid[half] = total
 
+    for half in (0, 1):
+        for way in (0, 1):
+            for by in range(NX):
+                if by in far_places[way]:
+                    first_copy(half, way, by).wait_send()
+                second_copy(half, way, by).wait_send()
+
     levels = gain_ref.shape[0]
     chosen = lax.broadcasted_iota(jnp.int32, (levels, 1), 0) == level_ref[0]
     gain_row = jnp.sum(jnp.where(chosen, gain_ref[...], 0.0), axis=0, keepdims=True)
@@ -359,39 +390,14 @@
             total = total + rx3[half, by - 1].astype(jnp.float32)
         out_ref[half * HALF:(half + 1) * HALF, :] = (total * gain_row).astype(jnp.bfloat16)
 
-    for kind in (KEY, VALUE, WEIGHT):
-        sibling_copy(kind, 0, 0).wait_send()
-        sibling_copy(kind, 0, 8).wait_send()
-        for way in (0, 1):
-            first_hop(kind, way).wait_send()
-            if kind == WEIGHT or kind == way:
-                far_copy(kind, way).wait_send()
-
-    def left(dist, _):
-        for kind in (KEY, VALUE, WEIGHT):
-            for way in (0, 1):
-                sibling_copy(kind, way, dist).wait_send()
-
-                @pl.when(dist < 7)
-                def _():
-                    ring_copy(kind, way, dist).wait_send()
-
-        return 0
-
-    lax.fori_loop(1, 8, left, 0)
     for half in (0, 1):
-        for way in (0, 1):
-            for by in range(NX):
-                if by in far_places[way]:
-                    first_copy(half, way, by).wait_send()
-                second_copy(half, way, by).wait_send()
         for by in (1, 2, 3):
             third_copy(half, by).wait_send()
 
 
 def on_device(query_rows, key_rows, value_rows, block_mask, noise_level, level_gain, out_weight):
     vmem = pl.BlockSpec(memory_space=pltpu.VMEM)
-    hbm = pl.BlockSpec(memory_space=pl.ANY)
+    hbm = pl.BlockSpec(memory_space=pltpu.HBM)
     smem = pl.BlockSpec(memory_space=pltpu.SMEM)
     dma = pltpu.SemaphoreType.DMA
     tokens = 2 * NZ * ROWS

time: 101 us -> 100 us (0.990)
  no operation moved by 1% of the time
where the time goes in v3:
time: 100 us
  Pallas kernels  97.9 us (98%)
  local copies, waits for them, and re-layouts  1.56 us (2%)
    pallas_call x1, Pallas kernels, on_device(): pl.pallas_call(kernel, out_shape=jax.ShapeDtypeStruct((ROWS, WIDTH), jnp....  97.9 us

profile of v3, /device:TPU:6, one launch (start us, length us, event | category | flops | bytes accessed | tf_op | source)
XLA Modules:
  0.0 100.2 jit_solution(14381327381433269027)
XLA Ops:
  0.7 97.9 %shard_map.73 = bf16[160,384]{1,0:T(8,128)(2,1)} custom-call(bf16[160,384]{1,0:T(8,128)(2,1)} %q_hbm.1, bf16[160,384]{1,0:T(8,128)(2,1)} %k_hbm.1, bf16[160,384]{1,0:T(8,128)(2,1)} %v_hbm.1, s32[1,32]{1,0:T(1,128)} %mask_ref.1, s32[1]{0:T(128)S(6)} %copy.9.level_ref, f32[16,384]{1,0:T(8,128)} %gain_hbm.1, bf16[192,384]{1,0:T(8,128)(2,1)} %bitcast.1), custom_call_target="tpu_custom_call" | custom-call | tf_op jit(solution)/shard_map/pallas_call | solution.py:411
  98.6 1.6 %copy.10 = bf16[160,384]{1,0:T(8,128)(2,1)} copy(bf16[160,384]{1,0:T(8,128)(2,1)} %shard_map.73) | data formatting | bytes 245760

commit v4 on v3

--- a/solution.py
+++ b/solution.py
@@ -245,7 +245,8 @@
     sibling_arrival(VALUE, 0, 8).wait_recv()
     attend(chunk_base(0, 8), [visible(z - 8, core), visible(z - 8, 1 - core)])
     for head in range(HEADS):
-        att[:, head * HD:(head + 1) * HD] = (acc[head] / row_sum[head]).astype(jnp.bfloat16)
+        per_row = 1.0 / row_sum[head][:, 0:1]
+        att[:, head * HD:(head + 1) * HD] = (acc[head] * per_row).astype(jnp.bfloat16)
 
     for way in (0, 1):
         far_copy(WEIGHT, way).wait_recv()

time: 100 us -> 101 us (1.010)
  no operation moved by 1% of the time
where the time goes in v4:
time: 101 us; the launch traced here: 100 us
  Pallas kernels  98.1 us (97%)
  local copies, waits for them, and re-layouts  1.56 us (2%)
    pallas_call x1, Pallas kernels, on_device(): pl.pallas_call(kernel, out_shape=jax.ShapeDtypeStruct((ROWS, WIDTH), jnp....  98.1 us

profile of v4, /device:TPU:6, one launch (start us, length us, event | category | flops | bytes accessed | tf_op | source)
XLA Modules:
  0.0 100.4 jit_solution(4397936658697054735)
XLA Ops:
  0.7 98.1 %shard_map.73 = bf16[160,384]{1,0:T(8,128)(2,1)} custom-call(bf16[160,384]{1,0:T(8,128)(2,1)} %q_hbm.1, bf16[160,384]{1,0:T(8,128)(2,1)} %k_hbm.1, bf16[160,384]{1,0:T(8,128)(2,1)} %v_hbm.1, s32[1,32]{1,0:T(1,128)} %mask_ref.1, s32[1]{0:T(128)S(6)} %copy.9.level_ref, f32[16,384]{1,0:T(8,128)} %gain_hbm.1, bf16[192,384]{1,0:T(8,128)(2,1)} %bitcast.1), custom_call_target="tpu_custom_call" | custom-call | tf_op jit(solution)/shard_map/pallas_call | solution.py:412
  98.8 1.6 %copy.10 = bf16[160,384]{1,0:T(8,128)(2,1)} copy(bf16[160,384]{1,0:T(8,128)(2,1)} %shard_map.73) | data formatting | bytes 245760
